TPU v7x, 32 devices: a whole 2x2x4 slice. The times are simulated.
32 devices in a mesh: src: 8 (over z, y), att: 4 (over x, core).
Axes of the slice: x: 2, y: 2, z: 4, core: 2. Of those that a mesh axis runs over, the one named last changes fastest.
Arguments:
- astro: float32 [5, 4096], P(None, 'src'), may hold values from -6 to 6
- attitude: float32 [196608], P('att'), may hold values from -6 to 6
- spline_weights: bfloat16 [2048, 64, 128], P(('src', 'att')), may hold values from -0.75 to 0.75
- source_coeffs: bfloat16 [2048, 5, 128], P(('src', 'att')), may hold values from -2.5 to 2.5
- observations: float32 [2048, 128], P(('src', 'att')), may hold values from -12 to 12
- knot_start: int32 [2048], P(('src', 'att')), may hold values from 0 to 49088
- block_count: int32 [4, 32], P('att', 'src'), may hold values from 1 to 16, as said below
Outputs:
- astro_new: float32 [5, 4096], P(None, 'src')
- attitude_new: float32 [196608], P('att')
Inputs may be any that keep to these rules, and one draw needn't show every extreme that they name: `block_count`: A block's live tiles fill its slots 0 to count - 1 at that owner; the other slots hold entries that no output reads. Some block has all 16 slots live.
All inputs are finite; a program needn't handle non-finite values.
Results may differ from a plain program's by a relative error of at most 0.0003.
Values sent between devices are 32-bit elements; how exact they have to be, the bound alone decides.
A program may use at most 64 MiB of HBM per device.

v0:
```python
import jax
import jax.numpy as jnp
from jax import lax
from jax.sharding import PartitionSpec as P

PASSES = 2


damping = 1.0


def attitude_model(weights, window):
    return jnp.sum(weights.astype(jnp.float32) * window[..., None], axis=-2)


def source_model(coeffs, params):
    return jnp.sum(coeffs.astype(jnp.float32) * params, axis=-2)


def local(astro, attitude, spline_weights, source_coeffs, observations, knot_start, block_count):
    blocks = block_count.shape[1]
    param_count = astro.shape[0]
    block_rows = astro.shape[1] // blocks
    slot_count = spline_weights.shape[0] // blocks
    knot_count = spline_weights.shape[1]
    knot_att = attitude.shape[0]
    weights = spline_weights.reshape(blocks, slot_count, knot_count, block_rows)
    coeffs = source_coeffs.reshape(blocks, slot_count, param_count, block_rows)
    observed = observations.reshape(blocks, slot_count, block_rows)
    starts = knot_start.reshape(blocks, slot_count)
    counts = block_count[0]
    tile_data = (weights, coeffs, observed, starts)
    offsets = jnp.arange(knot_count, dtype=jnp.int32)

    def over_slots(step_fn, totals):
        return step_fn(totals, tile_data, 0)

    def live_mask(slot_first, width):
        slot_ids = slot_first + jnp.arange(width, dtype=jnp.int32)
        return (slot_ids[None, :] < counts[:, None]).astype(jnp.float32)

    def residual(tile_part, slot_first, params, attitude_now):
        part_w, part_c, part_y, part_s = tile_part
        live = live_mask(slot_first, part_w.shape[1])
        window = attitude_now[part_s[..., None] + offsets]
        predicted = source_model(part_c, params[:, None]) + attitude_model(part_w, window)
        return (part_y - predicted) * live[..., None]

    def diag_step(totals, tile_part, slot_first):
        part_w, part_c, part_y, part_s = tile_part
        live = live_mask(slot_first, part_w.shape[1])
        source_sq = jnp.sum(jnp.square(part_c.astype(jnp.float32)) * live[:, :, None, None], axis=1)
        knot_sq = jnp.sum(jnp.square(part_w.astype(jnp.float32)), axis=-1) * live[:, :, None]
        return (source_sq, totals[1].at[part_s[..., None] + offsets].add(knot_sq))

    source_zero = jnp.zeros((blocks, param_count, block_rows), jnp.float32)
    knot_zero = jnp.zeros((knot_att,), jnp.float32)
    source_part, knot_part = over_slots(diag_step, (source_zero, knot_zero))
    source_diag = lax.psum(source_part, "att") + damping
    knot_diag = lax.psum(knot_part, "src") + damping
    params = jnp.transpose(astro.reshape(param_count, blocks, block_rows), (1, 0, 2))
    attitude_now = attitude
    for pass_no in range(PASSES):
        params_old = params
        attitude_old = attitude_now

        def source_step(totals, tile_part, slot_first):
            resid = residual(tile_part, slot_first, params_old, attitude_old)
            return jnp.sum(tile_part[1].astype(jnp.float32) * resid[:, :, None, :], axis=1)

        gradient = over_slots(source_step, source_zero)
        gradient = lax.psum(gradient, "att")
        params = params_old + gradient / source_diag
        params_new = params

        def knot_step(totals, tile_part, slot_first):
            resid = residual(tile_part, slot_first, params_new, attitude_old)
            values = jnp.sum(tile_part[0].astype(jnp.float32) * resid[:, :, None, :], axis=-1)
            return totals.at[tile_part[3][..., None] + offsets].add(values)

        knot_terms = over_slots(knot_step, knot_zero)
        knot_terms = lax.psum(knot_terms, "src")
        attitude_now = attitude_old + knot_terms / knot_diag
    astro_new = jnp.transpose(params, (1, 0, 2)).reshape(param_count, blocks * block_rows)
    return (astro_new, attitude_now)


def solution(mesh):
    placed = (
        P(None, "src"),
        P("att"),
        P(("src", "att"), None, None),
        P(("src", "att"), None, None),
        P(("src", "att"), None),
        P(("src", "att")),
        P("att", "src"),
    )
    return jax.shard_map(
        local, mesh=mesh, in_specs=placed, out_specs=(P(None, "src"), P("att")), check_vma=False
    )
```

profile of v0, /device:TPU:0, one launch (start us, length us, event | category | flops | bytes accessed | tf_op | source)
XLA Modules:
  0.0 318.1 jit_solution(2408341965380640918)
XLA Ops:
  7.2 0.0 all-reduce.7.cloned.1.call-start
  7.2 0.7 fusion.14
  7.9 0.1 reshape.180
  8.0 0.7 add.83
  8.8 0.7 reshape.177
  9.5 0.1 compare_select_fusion
  9.6 0.1 reshape.183
  9.6 0.0 copy-start.1
  9.7 19.6 %gather_fusion = f32[4096]{0:T(1024)S(1)} fusion(f32[49152]{0:T(1024)} %param.8, s32[4096]{0:T(1024)S(1)} %broadcast_clamp_fusion), kind=kCustom, calls=%fused_computation | custom fusion | bytes 49152 | tf_op jit(solution)/shard_map/gather | solution.py:45
  29.2 0.0 copy-start.2
  29.3 0.0 copy-start.4
  29.3 0.1 mul.164
  29.3 0.0 copy-done.1
  29.3 0.7 fusion
  30.0 0.1 copy-done.2
  30.2 0.0 copy-done.4
  30.2 0.1 broadcast_multiply_fusion.2
  30.3 0.1 multiply_reduce_fusion.1
  30.4 12.8 %all-reduce.1 = (f32[4,5,128]{2,0,1:T(4,128)S(1)}, f32[4,5,128]{2,0,1:T(4,128)S(1)}) all-reduce(f32[4,5,128]{2,0,1:T(4,128)S(1)} %get-tuple-element.5, f32[4,5,128]{2,0,1:T(4,128)S(1)} %get-tuple-element.4), channel_id=1, replica_groups=mesh['src'=8,'att'=4] {'att'}, use_global_device_ids=true, to_apply=%region_3.0 | all-reduce | flops 5120 | bytes 40960 | tf_op jit(solution)/shard_map/psum | solution.py:72
  43.2 0.1 subtract_multiply_fusion.1
  43.3 0.0 copy-start
  43.3 1.2 fusion.2
  44.4 0.1 broadcast_multiply_fusion
  44.5 0.1 reshape.209
  44.6 0.1 reshape.201
  44.7 29.2 %scatter_custom_fusion = f32[49152]{0:T(1024)} fusion(s32[4096]{0:T(1024)S(1)} %reshape.183, f32[4096]{0:T(1024)S(1)} %reshape.201, f32[]{:T(128)} %constant.4.clone.1), kind=kCustom, calls=%fused_computation.30 | custom fusion | flops 4096 | bytes 196612 | tf_op jit(solution)/shard_map/scatter-add | solution.py:79
  73.9 29.2 %scatter_custom_fusion.1 = f32[49152]{0:T(1024)} fusion(s32[4096]{0:T(1024)S(1)} %reshape.183, f32[4096]{0:T(1024)S(1)} %reshape.209, f32[]{:T(128)} %constant.4.clone.1), kind=kCustom, calls=%fused_computation.28 | custom fusion | flops 4096 | bytes 196612 | tf_op jit(solution)/shard_map/scatter-add | solution.py:54
  103.1 0.0 all-reduce.7.cloned.1.call-update
  103.1 0.0 all-reduce.5.cloned.1.call-start
  103.1 71.9 %all-reduce.7.cloned.1.call-done = (f32[49152]{0:T(1024)}, f32[49152]{0:T(1024)}) async-done(((f32[49152]{0:T(1024)}, f32[49152]{0:T(1024)}), (f32[49152]{0:T(1024)}, f32[49152]{0:T(1024)})) %all-reduce.7.cloned.1.call-update) | async-done | bytes 393232 | tf_op jit(solution)/shard_map/psum | solution.py:82
  175.1 0.0 copy-done
  175.1 1.1 divide_add_fusion.1
  176.1 23.0 %gather_fusion.1 = f32[4096]{0:T(1024)S(1)} fusion(f32[49152]{0:T(1024)S(1)} %divide_add_fusion.1, s32[4096]{0:T(1024)S(1)} %broadcast_clamp_fusion), kind=kCustom, calls=%fused_computation.1 | custom fusion | bytes 49152 | tf_op jit(solution)/shard_map/gather | solution.py:45
  199.2 0.1 mul.182
  199.2 0.7 fusion.3
  200.0 0.0 copy-start.3
  200.0 0.1 broadcast_multiply_fusion.1
  200.1 10.1 %psum.46 = f32[4,5,128]{2,0,1:T(4,128)S(1)} all-reduce(f32[4,5,128]{2,0,1:T(4,128)S(1)} %multiply_reduce_fusion), channel_id=1, replica_groups=mesh['src'=8,'att'=4] {'att'}, use_global_device_ids=true, to_apply=%region_15.0 | all-reduce | flops 2560 | bytes 20480 | tf_op jit(solution)/shard_map/psum | solution.py:72
  210.3 0.1 subtract_multiply_fusion
  210.3 0.6 fusion.4
  211.0 0.1 reshape.217
  211.0 29.2 %scatter_custom_fusion.2 = f32[49152]{0:T(1024)} fusion(s32[4096]{0:T(1024)S(1)} %reshape.183, f32[4096]{0:T(1024)S(1)} %reshape.217, f32[]{:T(128)} %constant.4.clone.1), kind=kCustom, calls=%fused_computation.26 | custom fusion | flops 4096 | bytes 196612 | tf_op jit(solution)/shard_map/scatter-add | solution.py:79
  240.2 0.0 all-reduce.5.cloned.1.call-update
  240.3 0.6 copy.11
  240.9 68.8 %all-reduce.5.cloned.1.call-done = f32[49152]{0:T(1024)} async-done(((f32[49152]{0:T(1024)}), f32[49152]{0:T(1024)}) %all-reduce.5.cloned.1.call-update) | async-done | bytes 196624 | tf_op jit(solution)/shard_map/psum | solution.py:82
  309.6 0.0 copy-done.3
  309.6 1.6 divide_add_fusion
  (9 shorter events, 0.2 us)
Async XLA Ops:
  7.2 167.9 %all-reduce.7.cloned.1.call-start = ((), (), s32[]{:S(2)}) async-start(), calls=%async_computation.1 | async-start | bytes 786432 | tf_op jit(solution)/shard_map/psum | solution.py:82
  9.6 19.7 %copy-start.1 = (bf16[64,64,128]{2,1,0:T(8,128)(2,1)S(1)}, bf16[64,64,128]{2,1,0:T(8,128)(2,1)}, u32[]{:S(2)}) copy-start(bf16[64,64,128]{2,1,0:T(8,128)(2,1)} %param.9) | copy-start | bytes 3145732
  29.2 0.9 copy-start.2
  29.3 0.9 copy-start.4
  43.3 131.8 %copy-start = (f32[49152]{0:T(1024)S(1)}, f32[49152]{0:T(1024)}, u32[]{:S(2)}) copy-start(f32[49152]{0:T(1024)} %param.8) | copy-start | bytes 589828
  103.1 206.5 %all-reduce.5.cloned.1.call-start = ((), (), s32[]{:S(2)}) async-start(), calls=%async_computation | async-start | bytes 393216 | tf_op jit(solution)/shard_map/psum | solution.py:82
  200.0 109.7 %copy-start.3 = (f32[49152]{0:T(1024)S(1)}, f32[49152]{0:T(1024)}, u32[]{:S(2)}) copy-start(f32[49152]{0:T(1024)} %get-tuple-element.7) | copy-start | bytes 589828
Sparse Core Ops, SparseCore 0:
  103.2 71.8 all-reduce.6
  240.4 69.2 all-reduce.4
where the time goes:
time: 318 us
  waiting for transfers between devices  141 us (44%)
  other arithmetic  94.9 us (30%)
  local copies, waits for them, and re-layouts  45.3 us (14%)
  blocking collectives  22.9 us (7%)
  between operations  14.2 us (4%)
    psum x2, waiting for transfers between devices, local(): knot_terms = lax.psum(knot_terms, 'src')  141 us
    scatter-add x2, other arithmetic, knot_step(): return totals.at[tile_part[3][..., None] + offsets].add(values)  58.4 us
    gather x2, local copies, waits for them, and re-layouts, residual(): window = attitude_now[part_s[..., None] + offsets]  42.6 us
    scatter-add x1, other arithmetic, diag_step(): return (source_sq, totals[1].at[part_s[..., None] + offsets].add(knot_sq))  29.2 us
    psum x2, blocking collectives, local(): gradient = lax.psum(gradient, 'att')  22.9 us
  transfers between devices with their start and end apart: 2, of which 2 were waited for; matrix products, arithmetic and copies ran while one was open for 0% of the time, Pallas kernels for 0%

commit v1 on v0

v1 whole, which is shorter than its diff:
```python
import functools

import jax
import jax.numpy as jnp
from jax import lax
from jax.experimental import pallas as pl
from jax.experimental.pallas import tpu as pltpu
from jax.sharding import PartitionSpec as P

PASSES = 2
LANES = 128
GROUP = 4

damping = 1.0

F32 = jnp.float32
BF16 = jnp.bfloat16
MESH = pl.DeviceIdType.MESH


def split(value):
    high = value.astype(BF16)
    low = (value - high.astype(F32)).astype(BF16)
    return high, low


def dot(a, b):
    return jnp.dot(a, b, preferred_element_type=F32)


def dot_rows(a, b):
    return lax.dot_general(a, b, (((1,), (1,)), ((), ())), preferred_element_type=F32)


def kernel(
    n_src, n_att, blocks, slots, knots, params, rows,
    astro_ref, attitude_ref, w_ref, c_ref, y_ref, start_ref, count_ref,
    x_out, a_out,
    planes, coeffs32, hot, pick, offs, starts, acc, inv, att_first, att_later, sq_buf, grad_buf,
    att_send, att_recv, src_send, src_recv,
):
    tiles = blocks * slots
    wide = slots * knots
    src = lax.axis_index("src")
    att = lax.axis_index("att")

    barrier = pltpu.get_barrier_semaphore()

    def greet_src(step, carry):
        pl.semaphore_signal(barrier, inc=1, device_id=(lax.rem(src + step, n_src), att), device_id_type=MESH)
        return carry

    def greet_att(step, carry):
        pl.semaphore_signal(barrier, inc=1, device_id=(src, lax.rem(att + step, n_att)), device_id_type=MESH)
        return carry

    lax.fori_loop(1, n_att, greet_att, 0)
    lax.fori_loop(1, n_src, greet_src, 0)

    def send_src(buf, which):
        def step_fn(step, carry):
            pltpu.make_async_remote_copy(
                src_ref=buf.at[src], dst_ref=buf.at[src],
                send_sem=src_send.at[which], recv_sem=src_recv.at[which],
                device_id=(lax.rem(src + step, n_src), att), device_id_type=MESH,
            ).start()
            return carry

        lax.fori_loop(1, n_src, step_fn, 0)

    def send_att(buf, which):
        def step_fn(step, carry):
            pltpu.make_async_remote_copy(
                src_ref=buf.at[att], dst_ref=buf.at[att],
                send_sem=att_send.at[which], recv_sem=att_recv.at[which],
                device_id=(src, lax.rem(att + step, n_att)), device_id_type=MESH,
            ).start()
            return carry

        lax.fori_loop(1, n_att, step_fn, 0)

    def wait_bytes(buf, count, sem):
        part = buf.at[pl.ds(0, count)]
        pltpu.make_async_copy(part, part, sem).wait()

    row_starts = start_ref[...]
    twice = jnp.broadcast_to(jnp.concatenate([row_starts, row_starts], axis=1), (8, LANES))
    starts[src] = twice
    column = jnp.transpose(twice)[0:tiles, 0:1]
    start = jnp.broadcast_to(column, (tiles, LANES))
    off = jnp.bitwise_and(start, LANES - 1)
    lane = lax.broadcasted_iota(jnp.int32, (tiles, LANES), 1)
    start_row = jnp.broadcast_to(jnp.right_shift(column, 7), (tiles, rows))
    row_id = lax.broadcasted_iota(jnp.int32, (tiles, rows), 1)
    pick[0:tiles, :] = jnp.where(row_id == start_row, 1.0, 0.0).astype(BF16)
    pick[tiles:, :] = jnp.where(row_id == start_row + 1, 1.0, 0.0).astype(BF16)

    coeffs32[:, 0:params, :] = c_ref[...].astype(F32)
    for p in range(params):
        planes[p] = coeffs32[:, p, :]

    slot_id = lax.broadcasted_iota(jnp.int32, (slots, LANES), 0)
    live = [slot_id < count_ref[0, b] for b in range(blocks)]
    own = jnp.right_shift(lax.broadcasted_iota(jnp.int32, (slots, wide), 1), 6) == lax.broadcasted_iota(
        jnp.int32, (slots, wide), 0
    )

    def windows(attitude):
        high, low = split(attitude)
        found = dot(pick[...], jnp.concatenate([high, low], axis=1))
        found = found[:, :LANES] + found[:, LANES:]
        window = jnp.where(lane >= off, found[:tiles], found[tiles:])
        for bit in range(7):
            moved = pltpu.roll(window, LANES - (1 << bit), 1)
            window = jnp.where(jnp.bitwise_and(off, 1 << bit) != 0, moved, window)
        return jnp.where(lane < knots, window, pltpu.roll(window, knots, 1))

    def predict(window):
        found = []
        for b in range(blocks):
            part = window[b * slots : (b + 1) * slots]
            part = jnp.where(own, jnp.concatenate([part] * (wide // LANES), axis=1), 0.0)
            both = dot(jnp.concatenate(split(part), axis=0), w_ref[b * wide : (b + 1) * wide, :])
            found.append(both[:slots] + both[slots:])
        return found

    def residual(x, predicted):
        found = []
        for b in range(blocks):
            total = predicted[b]
            for p in range(params):
                total = total + planes[p, b * slots : (b + 1) * slots, :] * x[p * blocks + b : p * blocks + b + 1, :]
            found.append(jnp.where(live[b], y_ref[b * slots : (b + 1) * slots, :] - total, 0.0))
        return found

    def source_terms(resid):
        return [
            jnp.sum(planes[p, b * slots : (b + 1) * slots, :] * resid[b], axis=0, keepdims=True)
            for p in range(params)
            for b in range(blocks)
        ]

    def source_squares():
        return [
            jnp.sum(jnp.where(live[b], jnp.square(planes[p, b * slots : (b + 1) * slots, :]), 0.0), axis=0, keepdims=True)
            for p in range(params)
            for b in range(blocks)
        ]

    def own_columns(both):
        both = jnp.where(own, both[:slots] + both[slots:], 0.0)
        total = both[:, :LANES]
        for part in range(1, wide // LANES):
            total = total + both[:, part * LANES : (part + 1) * LANES]
        return total + pltpu.roll(total, knots, 1)

    def placed(values):
        values = jnp.concatenate(values, axis=0)
        for bit in range(6):
            moved = pltpu.roll(values, 1 << bit, 1)
            values = jnp.where(jnp.bitwise_and(off, 1 << bit) != 0, moved, values)
        half = tiles // 2
        return jnp.where(lane[:half] < knots, values[:half], values[half:])

    def knot_terms(resid):
        return [
            own_columns(dot_rows(jnp.concatenate(split(resid[b]), axis=0), w_ref[b * wide : (b + 1) * wide, :]))
            for b in range(blocks)
        ]

    def knot_squares():
        ones = jnp.ones((slots, LANES), BF16)
        found = []
        for b in range(blocks):
            high, low = split(jnp.square(w_ref[b * wide : (b + 1) * wide, :].astype(F32)))
            both = jnp.concatenate([dot_rows(ones, high), dot_rows(ones, low)], axis=0)
            found.append(jnp.where(live[b], own_columns(both), 0.0))
        return found

    def prepare(chunk, carry):
        first = chunk * GROUP
        low_half = lax.broadcasted_iota(jnp.int32, (8, LANES), 1) < tiles
        ids = lax.broadcasted_iota(jnp.int32, (rows, LANES), 0)
        for pair in range(GROUP // 2):
            both = jnp.where(low_half, starts[first + 2 * pair], starts[first + 2 * pair + 1])
            both = jnp.broadcast_to(jnp.right_shift(both, 7)[0:1], (rows, LANES))
            hot[chunk, :, pair * LANES : (pair + 1) * LANES] = jnp.where(ids == both, 1.0, 0.0).astype(BF16)
        for d in range(GROUP):
            lanes_of = jnp.transpose(jnp.bitwise_and(starts[first + d], LANES - 1))
            offs[first + d] = jnp.broadcast_to(lanes_of[0:tiles, 0:1], (tiles, LANES))
        return carry

    def group_sum(chunk, buf_of):
        first = chunk * GROUP
        half = tiles // 2
        parts = []
        for d in range(GROUP):
            packed = buf_of(first + d)
            other = pltpu.roll(packed, knots, 1)
            low_half = lane[:half] < knots
            values = jnp.concatenate([jnp.where(low_half, packed, other), jnp.where(low_half, other, packed)], axis=0)
            at = offs[first + d]
            here = jnp.where(jnp.logical_and(lane >= at, lane < at + knots), values, 0.0)
            later = jnp.where(lane < at - knots, values, 0.0)
            parts.append(jnp.concatenate([here, later], axis=1))
        high, low = split(jnp.concatenate(parts, axis=0))
        return dot(hot[chunk], high) + dot(hot[chunk], low)

    n_groups = n_src // GROUP

    def over_groups(buf_of):
        if n_groups <= 2:
            total = group_sum(0, buf_of)
            for chunk in range(1, n_groups):
                total = total + group_sum(chunk, buf_of)
        else:
            acc[...] = jnp.zeros_like(acc)

            def step_fn(chunk, carry):
                acc[...] += group_sum(chunk, buf_of)
                return carry

            lax.fori_loop(0, n_groups, step_fn, 0)
            total = acc[...]
        return total[:, :LANES] + pltpu.roll(total[:, LANES:], 1, 0)

    x = jnp.concatenate(
        [astro_ref[p : p + 1, b * LANES : (b + 1) * LANES] for p in range(params) for b in range(blocks)], axis=0
    )
    count = params * blocks
    attitude = attitude_ref[...]
    for turn in range(PASSES):
        predicted = predict(windows(attitude))
        terms = source_terms(residual(x, predicted))
        if turn == 0:
            att_first[att] = jnp.concatenate(terms + source_squares(), axis=0)
            pl.semaphore_wait(barrier, n_src + n_att - 2)
            send_att(att_first, 0)
            send_src(starts, 0)
            sq_buf[src] = placed(knot_squares())
            send_src(sq_buf, 1)
            wait_bytes(att_first, n_att - 1, att_recv.at[0])
            total = att_first[0]
            for j in range(1, n_att):
                total = total + att_first[j]
            source_inv = 1.0 / (total[count:] + damping)
            total = total[:count]
        else:
            pad = jnp.zeros((att_later.shape[2] - count, LANES), F32)
            att_later[turn - 1, att] = jnp.concatenate(terms + [pad], axis=0)
            send_att(att_later.at[turn - 1], turn)
            wait_bytes(att_later.at[turn - 1], n_att - 1, att_recv.at[turn])
            total = att_later[turn - 1, 0]
            for j in range(1, n_att):
                total = total + att_later[turn - 1, j]
            total = total[:count]
        x = x + total * source_inv
        grad_buf[turn, src] = placed(knot_terms(residual(x, predicted)))
        send_src(grad_buf.at[turn], 2 + turn)
        if turn == 0:
            wait_bytes(starts, n_src - 1, src_recv.at[0])
            if n_groups <= 2:
                for chunk in range(n_groups):
                    prepare(chunk, 0)
            else:
                lax.fori_loop(0, n_groups, prepare, 0)
            wait_bytes(sq_buf, n_src - 1, src_recv.at[1])
            inv[...] = 1.0 / (over_groups(lambda d: sq_buf[d]) + damping)
        if turn == PASSES - 1:
            for p in range(params):
                for b in range(blocks):
                    n = p * blocks + b
                    x_out[p : p + 1, b * LANES : (b + 1) * LANES] = x[n : n + 1, :]
        wait_bytes(grad_buf.at[turn], n_src - 1, src_recv.at[2 + turn])
        attitude = attitude + over_groups(lambda d: grad_buf[turn, d]) * inv[...]
    a_out[...] = attitude

    wait_bytes(att_first, n_att - 1, att_send.at[0])
    wait_bytes(starts, n_src - 1, src_send.at[0])
    wait_bytes(sq_buf, n_src - 1, src_send.at[1])
    for turn in range(PASSES):
        wait_bytes(grad_buf.at[turn], n_src - 1, src_send.at[2 + turn])
        if turn:
            wait_bytes(att_later.at[turn - 1], n_att - 1, att_send.at[turn])


def local(n_src, n_att, astro, attitude, spline_weights, source_coeffs, observations, knot_start, block_count):
    blocks = block_count.shape[1]
    params = astro.shape[0]
    tiles, knots, block_rows = spline_weights.shape
    slots = tiles // blocks
    knot_att = attitude.shape[0]
    rows = knot_att // LANES
    count = params * blocks
    vmem = pl.BlockSpec(memory_space=pltpu.VMEM)
    smem = pl.BlockSpec(memory_space=pltpu.SMEM)
    x, a = pl.pallas_call(
        functools.partial(kernel, n_src, n_att, blocks, slots, knots, params, rows),
        out_shape=(
            jax.ShapeDtypeStruct(astro.shape, F32),
            jax.ShapeDtypeStruct((rows, LANES), F32),
        ),
        in_specs=[vmem] * 6 + [smem],
        out_specs=(vmem, vmem),
        scratch_shapes=[
            pltpu.VMEM((params, tiles, LANES), F32),
            pltpu.VMEM((tiles, 8, LANES), F32),
            pltpu.VMEM((n_src // GROUP, rows, GROUP * tiles), BF16),
            pltpu.VMEM((2 * tiles, rows), BF16),
            pltpu.VMEM((n_src, tiles, LANES), jnp.int32),
            pltpu.VMEM((n_src, 8, LANES), jnp.int32),
            pltpu.VMEM((rows, 2 * LANES), F32),
            pltpu.VMEM((rows, LANES), F32),
            pltpu.VMEM((n_att, 2 * count, LANES), F32),
            pltpu.VMEM((PASSES - 1, n_att, (count + 7) // 8 * 8, LANES), F32),
            pltpu.VMEM((n_src, tiles // 2, LANES), F32),
            pltpu.VMEM((PASSES, n_src, tiles // 2, LANES), F32),
            pltpu.SemaphoreType.DMA((PASSES,)),
            pltpu.SemaphoreType.DMA((PASSES,)),
            pltpu.SemaphoreType.DMA((PASSES + 2,)),
            pltpu.SemaphoreType.DMA((PASSES + 2,)),
        ],
        compiler_params=pltpu.CompilerParams(
            collective_id=0, has_side_effects=True, vmem_limit_bytes=40 * 1024 * 1024
        ),
    )(
        astro,
        attitude.reshape(rows, LANES),
        spline_weights.reshape(tiles * knots, block_rows),
        source_coeffs,
        observations,
        knot_start.reshape(1, tiles),
        block_count,
    )
    return (x, a.reshape(knot_att))


def solution(mesh):
    placed_as = (
        P(None, "src"),
        P("att"),
        P(("src", "att"), None, None),
        P(("src", "att"), None, None),
        P(("src", "att"), None),
        P(("src", "att")),
        P("att", "src"),
    )
    return jax.shard_map(
        functools.partial(local, mesh.shape["src"], mesh.shape["att"]),
        mesh=mesh, in_specs=placed_as, out_specs=(P(None, "src"), P("att")), check_vma=False,
    )
```

time: 318 us -> 31.9 us (0.10)
  waiting for transfers between devices: 141 us -> 0 us
  other arithmetic: 94.9 us -> 0 us
  local copies, waits for them, and re-layouts: 45.3 us -> 4.3 us
  Pallas kernels: 0 us -> 26.7 us
  blocking collectives: 22.9 us -> 0 us
  between operations: 14.2 us -> 0.71 us
    psum x2 -> x0, waiting for transfers between devices: 141 us -> none  [local(): knot_terms = lax.psum(knot_terms, 'src')]
    scatter-add x3 -> x0, other arithmetic: 87.6 us -> none  [the longest x2 58.4 us: knot_step(): return totals.at[tile_part[3][..., None] + offsets].add(values)]
    gather x2 -> x0, local copies, waits for them, and re-layouts: 42.6 us -> none  [residual(): window = attitude_now[part_s[..., None] + offsets]]
    pallas_call x0 -> x1, Pallas kernels: none -> 26.7 us  [local(): pl.pallas_call(functools.partial(kernel, n_src, n_att, blocks, slots, kno...]
    psum x2 -> x0, blocking collectives: 22.9 us -> none  [local(): gradient = lax.psum(gradient, 'att')]
    unnamed x11 -> x15, local copies, waits for them, and re-layouts: 0.72 us -> 4.3 us
    reduce_sum x9 -> x0, other arithmetic: 3.38 us -> none  [the longest x2 1.39 us: attitude_model(): return jnp.sum(weights.astype(jnp.float32) * window[..., None], axis=-2)]
  transfers between devices with their start and end apart: 2 -> 0, of which waited for: 2 -> 0; matrix products, arithmetic and copies ran while one was open for 0% -> 0% of each run, Pallas kernels for 0% -> 0%
where the time goes in v1:
time: 31.9 us; the launch traced here: 31.7 us
  Pallas kernels  26.7 us (84%)
  local copies, waits for them, and re-layouts  4.3 us (13%)
  between operations  0.71 us (2%)
    pallas_call x1, Pallas kernels, local(): pl.pallas_call(functools.partial(kernel, n_src, n_att, blocks, slots, kno...  26.7 us
    unnamed x15, local copies, waits for them, and re-layouts  4.3 us

profile of v1, /device:TPU:0, one launch (start us, length us, event | category | flops | bytes accessed | tf_op | source)
XLA Modules:
  0.0 31.7 jit_solution(2297010513124802107)
XLA Ops:
  0.6 0.0 copy-start.1
  0.6 0.0 copy-start.3
  0.7 0.0 copy-start.4
  0.7 0.0 copy-start.5
  0.7 1.0 %copy.9.c_ref = bf16[64,5,128]{2,1,0:T(8,128)(2,1)S(1)} copy(bf16[64,5,128]{2,0,1:T(8,128)(2,1)} %param.10) | data formatting | bytes 163840 | tf_op args[3]
  1.7 0.0 copy-done.1
  1.7 0.0 copy-done.3
  1.7 0.0 copy-done.4
  1.7 0.0 copy-done.5
  1.7 0.0 copy-start
  1.7 1.2 %copy-done = bf16[64,64,128]{2,1,0:T(8,128)(2,1)S(1)} copy-done((bf16[64,64,128]{2,1,0:T(8,128)(2,1)S(1)}, bf16[64,64,128]{2,1,0:T(8,128)(2,1)}, u32[]{:S(2)}) %copy-start) | copy-done | bytes 1048600
  2.9 0.0 copy-start.2
  3.0 0.8 %copy-done.2 = f32[64,128]{1,0:T(8,128)S(1)} copy-done((f32[64,128]{1,0:T(8,128)S(1)}, f32[64,128]{1,0:T(8,128)}, u32[]{:S(2)}) %copy-start.2) | copy-done | bytes 32792
  3.7 26.7 %shard_map.86 = (f32[5,512]{1,0:T(8,128)S(1)}, f32[384,128]{1,0:T(8,128)S(1)}) custom-call(f32[5,512]{1,0:T(8,128)S(1)} %copy-done.3, f32[384,128]{1,0:T(8,128)S(1)} %bitcast.5, bf16[4096,128]{1,0:T(8,128)(2,1)S(1)} %bitcast.4, bf16[64,5,128]{2,1,0:T(8,128)(2,1)S(1)} %copy.9.c_ref, f32[64,128]{1,0:T(8,128)S(1)} %copy-done.2, s32[1,64]{1,0:T(1,128)S(1)} %bitcast.7, ...), custom_call_target="tpu_custom_call" | custom-call | tf_op jit(solution)/shard_map/pallas_call | solution.py:297
  30.4 0.6 %copy.12 = f32[5,512]{1,0:T(8,128)} copy(f32[5,512]{1,0:T(8,128)S(1)} %get-tuple-element.8) | data formatting | bytes 20480
  31.0 0.7 %copy.13 = f32[49152]{0:T(1024)} copy(f32[49152]{0:T(1024)S(1)} %bitcast.6) | data formatting | bytes 393216
Async XLA Ops:
  0.6 1.1 %copy-start.1 = (f32[49152]{0:T(1024)S(1)}, f32[49152]{0:T(1024)}, u32[]{:S(2)}) copy-start(f32[49152]{0:T(1024)} %param.8) | copy-start | bytes 589828
  0.6 1.1 %copy-start.3 = (f32[5,512]{1,0:T(8,128)S(1)}, f32[5,512]{1,0:T(8,128)}, u32[]{:S(2)}) copy-start(f32[5,512]{1,0:T(8,128)} %astro_ref.1) | copy-start | bytes 30724
  0.7 1.1 %copy-start.4 = (s32[64]{0:T(128)S(1)}, s32[64]{0:T(128)}, u32[]{:S(2)}) copy-start(s32[64]{0:T(128)} %param.12) | copy-start | bytes 772
  0.7 1.1 %copy-start.5 = (s32[1,4]{1,0:T(1,128)S(1)}, s32[1,4]{1,0:T(1,128)}, u32[]{:S(2)}) copy-start(s32[1,4]{1,0:T(1,128)} %count_ref.1) | copy-start | bytes 52
  1.7 1.2 %copy-start = (bf16[64,64,128]{2,1,0:T(8,128)(2,1)S(1)}, bf16[64,64,128]{2,1,0:T(8,128)(2,1)}, u32[]{:S(2)}) copy-start(bf16[64,64,128]{2,1,0:T(8,128)(2,1)} %param.9) | copy-start | bytes 3145732
  2.9 0.8 %copy-start.2 = (f32[64,128]{1,0:T(8,128)S(1)}, f32[64,128]{1,0:T(8,128)}, u32[]{:S(2)}) copy-start(f32[64,128]{1,0:T(8,128)} %y_ref.1) | copy-start | bytes 98308

commit v2 on v1

--- a/solution.py
+++ b/solution.py
@@ -34,9 +34,10 @@
 
 def kernel(
     n_src, n_att, blocks, slots, knots, params, rows,
-    astro_ref, attitude_ref, w_ref, c_ref, y_ref, start_ref, count_ref,
-    x_out, a_out,
-    planes, coeffs32, hot, pick, offs, starts, acc, inv, att_first, att_later, sq_buf, grad_buf,
+    astro_hbm, attitude_hbm, w_hbm, c_hbm, y_hbm, start_hbm, count_hbm,
+    x_hbm, a_hbm,
+    astro_ref, attitude_ref, w_ref, c_ref, y_ref, start_ref, count_ref, x_out, a_out, load_sem, store_sem,
+    planes, hot, pick, offs, starts, acc, inv, att_buf, sq_buf, grad_buf,
     att_send, att_recv, src_send, src_recv,
 ):
     tiles = blocks * slots
@@ -46,6 +47,13 @@
 
     barrier = pltpu.get_barrier_semaphore()
 
+    def each(n, step_fn):
+        if n <= 8:
+            for step in sorted(range(1, n), key=lambda step: min(step, n - step)):
+                step_fn(step, 0)
+        else:
+            lax.fori_loop(1, n, step_fn, 0)
+
     def greet_src(step, carry):
         pl.semaphore_signal(barrier, inc=1, device_id=(lax.rem(src + step, n_src), att), device_id_type=MESH)
         return carry
@@ -54,8 +62,20 @@
         pl.semaphore_signal(barrier, inc=1, device_id=(src, lax.rem(att + step, n_att)), device_id_type=MESH)
         return carry
 
-    lax.fori_loop(1, n_att, greet_att, 0)
-    lax.fori_loop(1, n_src, greet_src, 0)
+    each(n_src, greet_src)
+    each(n_att, greet_att)
+
+    loads = [
+        pltpu.make_async_copy(there, here, load_sem.at[n])
+        for n, (there, here) in enumerate(
+            [
+                (start_hbm, start_ref), (attitude_hbm, attitude_ref), (w_hbm, w_ref), (c_hbm, c_ref),
+                (count_hbm, count_ref), (y_hbm, y_ref), (astro_hbm, astro_ref),
+            ]
+        )
+    ]
+    for load in loads:
+        load.start()
 
     def send_src(buf, which):
         def step_fn(step, carry):
@@ -66,7 +86,7 @@
             ).start()
             return carry
 
-        lax.fori_loop(1, n_src, step_fn, 0)
+        each(n_src, step_fn)
 
     def send_att(buf, which):
         def step_fn(step, carry):
@@ -77,12 +97,13 @@
             ).start()
             return carry
 
-        lax.fori_loop(1, n_att, step_fn, 0)
+        each(n_att, step_fn)
 
     def wait_bytes(buf, count, sem):
         part = buf.at[pl.ds(0, count)]
         pltpu.make_async_copy(part, part, sem).wait()
 
+    loads[0].wait()
     row_starts = start_ref[...]
     twice = jnp.broadcast_to(jnp.concatenate([row_starts, row_starts], axis=1), (8, LANES))
     starts[src] = twice
@@ -95,10 +116,7 @@
     pick[0:tiles, :] = jnp.where(row_id == start_row, 1.0, 0.0).astype(BF16)
     pick[tiles:, :] = jnp.where(row_id == start_row + 1, 1.0, 0.0).astype(BF16)
 
-    coeffs32[:, 0:params, :] = c_ref[...].astype(F32)
-    for p in range(params):
-        planes[p] = coeffs32[:, p, :]
-
+    loads[4].wait()
     slot_id = lax.broadcasted_iota(jnp.int32, (slots, LANES), 0)
     live = [slot_id < count_ref[0, b] for b in range(blocks)]
     own = jnp.right_shift(lax.broadcasted_iota(jnp.int32, (slots, wide), 1), 6) == lax.broadcasted_iota(
@@ -110,10 +128,12 @@
         found = dot(pick[...], jnp.concatenate([high, low], axis=1))
         found = found[:, :LANES] + found[:, LANES:]
         window = jnp.where(lane >= off, found[:tiles], found[tiles:])
-        for bit in range(7):
+        covered = jnp.bitwise_and(lane - off, LANES - 1) < knots
+        window = jnp.where(covered, window, pltpu.roll(window, knots, 1))
+        for bit in range(6):
             moved = pltpu.roll(window, LANES - (1 << bit), 1)
             window = jnp.where(jnp.bitwise_and(off, 1 << bit) != 0, moved, window)
-        return jnp.where(lane < knots, window, pltpu.roll(window, knots, 1))
+        return window
 
     def predict(window):
         found = []
@@ -224,36 +244,45 @@
             total = acc[...]
         return total[:, :LANES] + pltpu.roll(total[:, LANES:], 1, 0)
 
+    stores = [
+        pltpu.make_async_copy(x_out, x_hbm, store_sem.at[0]),
+        pltpu.make_async_copy(a_out, a_hbm, store_sem.at[1]),
+    ]
+    count = params * blocks
+    pad = jnp.zeros((att_buf.shape[2] - count, LANES), F32)
+
+    def att_total(which):
+        wait_bytes(att_buf.at[which], n_att - 1, att_recv.at[which])
+        total = att_buf[which, 0]
+        for j in range(1, n_att):
+            total = total + att_buf[which, j]
+        return total[:count]
+
+    loads[1].wait()
+    window = windows(attitude_ref[...])
+    for n in (2, 3, 5, 6):
+        loads[n].wait()
+    for p in range(params):
+        planes[p] = c_ref[p].astype(F32)
     x = jnp.concatenate(
         [astro_ref[p : p + 1, b * LANES : (b + 1) * LANES] for p in range(params) for b in range(blocks)], axis=0
     )
-    count = params * blocks
     attitude = attitude_ref[...]
     for turn in range(PASSES):
-        predicted = predict(windows(attitude))
+        predicted = predict(window)
         terms = source_terms(residual(x, predicted))
+        att_buf[turn, att] = jnp.concatenate(terms + [pad], axis=0)
         if turn == 0:
-            att_first[att] = jnp.concatenate(terms + source_squares(), axis=0)
             pl.semaphore_wait(barrier, n_src + n_att - 2)
-            send_att(att_first, 0)
+        send_att(att_buf.at[turn], turn)
+        if turn == 0:
+            att_buf[PASSES, att] = jnp.concatenate(source_squares() + [pad], axis=0)
+            send_att(att_buf.at[PASSES], PASSES)
             send_src(starts, 0)
             sq_buf[src] = placed(knot_squares())
             send_src(sq_buf, 1)
-            wait_bytes(att_first, n_att - 1, att_recv.at[0])
-            total = att_first[0]
-            for j in range(1, n_att):
-                total = total + att_first[j]
-            source_inv = 1.0 / (total[count:] + damping)
-            total = total[:count]
-        else:
-            pad = jnp.zeros((att_later.shape[2] - count, LANES), F32)
-            att_later[turn - 1, att] = jnp.concatenate(terms + [pad], axis=0)
-            send_att(att_later.at[turn - 1], turn)
-            wait_bytes(att_later.at[turn - 1], n_att - 1, att_recv.at[turn])
-            total = att_later[turn - 1, 0]
-            for j in range(1, n_att):
-                total = total + att_later[turn - 1, j]
-            total = total[:count]
+            source_inv = 1.0 / (att_total(PASSES) + damping)
+        total = att_total(turn)
         x = x + total * source_inv
         grad_buf[turn, src] = placed(knot_terms(residual(x, predicted)))
         send_src(grad_buf.at[turn], 2 + turn)
@@ -271,17 +300,22 @@
                 for b in range(blocks):
                     n = p * blocks + b
                     x_out[p : p + 1, b * LANES : (b + 1) * LANES] = x[n : n + 1, :]
+            stores[0].start()
         wait_bytes(grad_buf.at[turn], n_src - 1, src_recv.at[2 + turn])
         attitude = attitude + over_groups(lambda d: grad_buf[turn, d]) * inv[...]
+        if turn < PASSES - 1:
+            window = windows(attitude)
     a_out[...] = attitude
-
-    wait_bytes(att_first, n_att - 1, att_send.at[0])
+    stores[1].start()
+
     wait_bytes(starts, n_src - 1, src_send.at[0])
     wait_bytes(sq_buf, n_src - 1, src_send.at[1])
+    wait_bytes(att_buf.at[PASSES], n_att - 1, att_send.at[PASSES])
     for turn in range(PASSES):
+        wait_bytes(att_buf.at[turn], n_att - 1, att_send.at[turn])
         wait_bytes(grad_buf.at[turn], n_src - 1, src_send.at[2 + turn])
-        if turn:
-            wait_bytes(att_later.at[turn - 1], n_att - 1, att_send.at[turn])
+    for store in stores:
+        store.wait()
 
 
 def local(n_src, n_att, astro, attitude, spline_weights, source_coeffs, observations, knot_start, block_count):
@@ -292,42 +326,50 @@
     knot_att = attitude.shape[0]
     rows = knot_att // LANES
     count = params * blocks
-    vmem = pl.BlockSpec(memory_space=pltpu.VMEM)
-    smem = pl.BlockSpec(memory_space=pltpu.SMEM)
+    hbm = pl.BlockSpec(memory_space=pltpu.HBM)
     x, a = pl.pallas_call(
         functools.partial(kernel, n_src, n_att, blocks, slots, knots, params, rows),
         out_shape=(
             jax.ShapeDtypeStruct(astro.shape, F32),
             jax.ShapeDtypeStruct((rows, LANES), F32),
         ),
-        in_specs=[vmem] * 6 + [smem],
-        out_specs=(vmem, vmem),
+        in_specs=[hbm] * 7,
+        out_specs=(hbm, hbm),
         scratch_shapes=[
+            pltpu.VMEM(astro.shape, F32),
+            pltpu.VMEM((rows, LANES), F32),
+            pltpu.VMEM((tiles * knots, block_rows), BF16),
+            pltpu.VMEM((params, tiles, block_rows), BF16),
+            pltpu.VMEM((tiles, block_rows), F32),
+            pltpu.VMEM((1, tiles), jnp.int32),
+            pltpu.SMEM((1, blocks), jnp.int32),
+            pltpu.VMEM(astro.shape, F32),
+            pltpu.VMEM((rows, LANES), F32),
+            pltpu.SemaphoreType.DMA((7,)),
+            pltpu.SemaphoreType.DMA((2,)),
             pltpu.VMEM((params, tiles, LANES), F32),
-            pltpu.VMEM((tiles, 8, LANES), F32),
             pltpu.VMEM((n_src // GROUP, rows, GROUP * tiles), BF16),
             pltpu.VMEM((2 * tiles, rows), BF16),
             pltpu.VMEM((n_src, tiles, LANES), jnp.int32),
             pltpu.VMEM((n_src, 8, LANES), jnp.int32),
             pltpu.VMEM((rows, 2 * LANES), F32),
             pltpu.VMEM((rows, LANES), F32),
-            pltpu.VMEM((n_att, 2 * count, LANES), F32),
-            pltpu.VMEM((PASSES - 1, n_att, (count + 7) // 8 * 8, LANES), F32),
+            pltpu.VMEM((PASSES + 1, n_att, (count + 7) // 8 * 8, LANES), F32),
             pltpu.VMEM((n_src, tiles // 2, LANES), F32),
             pltpu.VMEM((PASSES, n_src, tiles // 2, LANES), F32),
-            pltpu.SemaphoreType.DMA((PASSES,)),
-            pltpu.SemaphoreType.DMA((PASSES,)),
+            pltpu.SemaphoreType.DMA((PASSES + 1,)),
+            pltpu.SemaphoreType.DMA((PASSES + 1,)),
             pltpu.SemaphoreType.DMA((PASSES + 2,)),
             pltpu.SemaphoreType.DMA((PASSES + 2,)),
         ],
         compiler_params=pltpu.CompilerParams(
-            collective_id=0, has_side_effects=True, vmem_limit_bytes=40 * 1024 * 1024
+            collective_id=0, has_side_effects=True, vmem_limit_bytes=60 * 1024 * 1024
         ),
     )(
         astro,
         attitude.reshape(rows, LANES),
         spline_weights.reshape(tiles * knots, block_rows),
-        source_coeffs,
+        jnp.transpose(source_coeffs, (1, 0, 2)),
         observations,
         knot_start.reshape(1, tiles),
         block_count,

time: 31.9 us -> 30.4 us (0.953)
  local copies, waits for them, and re-layouts: 4.3 us -> 2.94 us
    unnamed x15 -> x2, local copies, waits for them, and re-layouts: 4.3 us -> 2.94 us
where the time goes in v2:
time: 30.4 us; the launch traced here: 30.1 us
  Pallas kernels  26.5 us (87%)
  local copies, waits for them, and re-layouts  2.94 us (10%)
  between operations  0.64 us (2%)
    pallas_call x1, Pallas kernels, local(): pl.pallas_call(functools.partial(kernel, n_src, n_att, blocks, slots, kno...  26.5 us
    unnamed x2, local copies, waits for them, and re-layouts  2.94 us

profile of v2, /device:TPU:0, one launch (start us, length us, event | category | flops | bytes accessed | tf_op | source)
XLA Modules:
  0.0 30.1 jit_solution(345353599622805705)
XLA Ops:
  0.6 26.5 %shard_map.86 = (f32[5,512]{1,0:T(8,128)}, f32[384,128]{1,0:T(8,128)}) custom-call(f32[5,512]{1,0:T(8,128)} %astro_hbm.1, f32[384,128]{1,0:T(8,128)} %bitcast.6, bf16[4096,128]{1,0:T(8,128)(2,1)} %bitcast.5, bf16[5,64,128]{2,1,0:T(8,128)(2,1)} %bitcast.8, f32[64,128]{1,0:T(8,128)} %y_hbm.1, s32[1,64]{1,0:T(1,128)} %bitcast.9, s32[1,4]{1,0:T(1,128)} %count_hbm.1), custom_call_target="tpu_custom_call" | custom-call | tf_op jit(solution)/shard_map/pallas_call | solution.py:330
  27.2 1.3 %copy.11 = f32[5,512]{1,0:T(8,128)} copy(f32[5,512]{1,0:T(8,128)} %get-tuple-element.8) | data formatting | bytes 20480
  28.5 1.6 %copy.12 = f32[49152]{0:T(1024)} copy(f32[49152]{0:T(1024)} %bitcast.7) | data formatting | bytes 393216
